TPU v7x, 32 devices: a whole 2x2x4 slice. The times are simulated.
32 devices in a mesh: thick: 4 (over y, core), wide: 8 (over z, x).
Axes of the slice: x: 2, y: 2, z: 4, core: 2. Of those that a mesh axis runs over, the one named last changes fastest.
Arguments:
- phase_in: float32 [128, 512, 512], P('thick', 'wide'), may hold values from -1 to 1
- density_in: float32 [128, 512, 512], P('thick', 'wide'), may hold values from 0 to 1
Outputs:
- phase_out: float32 [128, 512, 512], P('thick', 'wide')
- density_out: float32 [128, 512, 512], P('thick', 'wide')
- mean_flux: float32 [], replicated
All inputs are finite; a program needn't handle non-finite values.
Results may differ from a plain program's by a relative error of at most 0.0001.
Values sent between devices are 32-bit elements; how exact they have to be, the bound alone decides.
A program may use at most 192 MiB of HBM per device.

v0:
```python
import math
import jax
import jax.numpy as jnp
from jax import lax
from jax.sharding import PartitionSpec as P

NX = 512
NY = 512
NZ = 128
DIFF_STEPS = 3
time_step = 100.0
stabilizer = 3.0
gradient_energy = 2.0
walk_step = 0.16


def with_halo(array, sides, width):
    for axis, dim in sides:
        peers, length = (lax.axis_size(axis), array.shape[dim])
        up = [(i, (i + 1) % peers) for i in range(peers)]
        down = [(j, i) for i, j in up]
        last = lax.slice_in_dim(array, length - width, length, axis=dim)
        leading = lax.slice_in_dim(array, 0, width, axis=dim)
        before = lax.ppermute(last, axis, up)
        after = lax.ppermute(leading, axis, down)
        array = jnp.concatenate([before, array, after], axis=dim)
    return array


def tables(length):
    index = jnp.arange(length, dtype=jnp.int32)
    folded = index[:, None] * index[None, :] % length
    angle = folded.astype(jnp.float32) * (2.0 * math.pi / length)
    return (jnp.cos(angle), jnp.sin(angle))


def squared_wave(index, length):
    signed = jnp.where(index < length // 2, index, index - length).astype(jnp.float32)
    return (signed * (2.0 * math.pi / length)) ** 2


def product(form, left, right):
    return jnp.einsum(form, left, right, precision=lax.Precision.HIGHEST)


def advance(density, conduct):
    centre = density[1:-1, 1:-1]
    middle = conduct[1:-1, 1:-1]

    def inflow(near_density, near_conduct):
        return 0.5 * (near_conduct + middle) * (near_density - centre)

    lower = inflow(density[:-2, 1:-1], conduct[:-2, 1:-1])
    total = lower + inflow(density[2:, 1:-1], conduct[2:, 1:-1])
    total = (
        total
        + inflow(density[1:-1, :-2], conduct[1:-1, :-2])
        + inflow(density[1:-1, 2:], conduct[1:-1, 2:])
    )
    total = (
        total
        + inflow(jnp.roll(centre, 1, 2), jnp.roll(middle, 1, 2))
        + inflow(jnp.roll(centre, -1, 2), jnp.roll(middle, -1, 2))
    )
    return (centre + walk_step * total, lower)


def per_device(phase_in, density_in):
    wide_count = lax.axis_size("wide")
    thick_count = lax.axis_size("thick")
    y_share = NY // wide_count
    x_share = NX // thick_count
    cosine_y, sine_y = tables(NY)
    cosine_x, sine_x = tables(NX)
    cosine_z, sine_z = tables(NZ)
    wave_y = squared_wave(
        lax.axis_index("wide") * y_share + jnp.arange(y_share, dtype=jnp.int32), NY
    )
    wave_x = squared_wave(
        lax.axis_index("thick") * x_share + jnp.arange(x_share, dtype=jnp.int32), NX
    )
    wave_z = squared_wave(jnp.arange(NZ, dtype=jnp.int32), NZ)
    wave = wave_y[:, None, None] + wave_z[None, :, None] + wave_x[None, None, :]
    implicit = 1.0 + time_step * stabilizer * wave + time_step * gradient_energy * wave * wave
    factor = 1.0 / (NX * NY * NZ)
    keep = (1.0 + time_step * stabilizer * wave) / implicit * factor
    drive = -time_step * wave / implicit * factor
    phase = phase_in
    chemical = phase * phase * phase - phase
    form = "fzxy,yk->fzxk"
    fields = jnp.stack([phase, chemical])
    real_part = product(form, fields, cosine_y)
    imag_part = -product(form, fields, sine_y)
    pair = (
        lax.all_to_all(real_part, "wide", split_axis=3, concat_axis=2, tiled=True),
        lax.all_to_all(imag_part, "wide", split_axis=3, concat_axis=2, tiled=True),
    )
    forward_real_part, forward_imag_part = pair
    form = "fzxy,xk->fzyk"
    out_real = product(form, forward_real_part, cosine_x) + product(form, forward_imag_part, sine_x)
    out_imag = product(form, forward_imag_part, cosine_x) - product(form, forward_real_part, sine_x)
    pair = (
        lax.all_to_all(out_real, "thick", split_axis=3, concat_axis=1, tiled=True),
        lax.all_to_all(out_imag, "thick", split_axis=3, concat_axis=1, tiled=True),
    )
    real_part, imag_part = pair
    form = "fzyk,zw->fywk"
    forward_out_real = product(form, real_part, cosine_z) + product(form, imag_part, sine_z)
    forward_out_imag = product(form, imag_part, cosine_z) - product(form, real_part, sine_z)
    real_part = forward_out_real
    imag_part = forward_out_imag
    new_real = keep * real_part[0] + drive * real_part[1]
    new_imag = keep * imag_part[0] + drive * imag_part[1]
    form = "ywk,wz->yzk"
    depth_real = product(form, new_real, cosine_z) - product(form, new_imag, sine_z)
    depth_imag = product(form, new_imag, cosine_z) + product(form, new_real, sine_z)
    real_part = lax.all_to_all(depth_real, "thick", split_axis=1, concat_axis=2, tiled=True)
    imag_part = lax.all_to_all(depth_imag, "thick", split_axis=1, concat_axis=2, tiled=True)
    form = "yzk,kx->zxy"
    out_real = product(form, real_part, cosine_x) - product(form, imag_part, sine_x)
    out_imag = product(form, imag_part, cosine_x) + product(form, real_part, sine_x)
    pair = (out_real, out_imag)
    real_part = lax.all_to_all(pair[0], "wide", split_axis=1, concat_axis=2, tiled=True)
    imag_part = lax.all_to_all(pair[1], "wide", split_axis=1, concat_axis=2, tiled=True)
    form = "zxk,ky->zxy"
    phase = product(form, real_part, cosine_y) - product(form, imag_part, sine_y)
    conduct = 0.05 + 0.95 * jax.nn.sigmoid(4.0 * phase)
    position = lax.axis_index("thick")
    final = thick_count - 1

    def pin_density(density, margin):
        depth = density.shape[0]
        layer = jnp.arange(depth, dtype=jnp.int32)[:, None, None]
        density = jnp.where((position == 0) & (layer < margin), 1.0, density)
        return jnp.where((position == final) & (layer >= depth - margin), 0.0, density)

    density = density_in
    lower = jnp.zeros_like(density)
    conduct_ext = with_halo(conduct, (("thick", 0), ("wide", 1)), 1)
    depth = conduct_ext.shape[0]
    layer = jnp.arange(depth, dtype=jnp.int32)[:, None, None]
    first = conduct_ext[1 : 1 + 1]
    last = conduct_ext[depth - 1 - 1 : depth - 1]
    conduct_ext = jnp.where((position == 0) & (layer < 1), first, conduct_ext)
    conduct_ext = jnp.where((position == final) & (layer >= depth - 1), last, conduct_ext)
    for turn in range(DIFF_STEPS):
        padded = pin_density(with_halo(density, (("thick", 0), ("wide", 1)), 1), 1)
        density, lower = advance(padded, conduct_ext)
    flux = lax.psum(jnp.sum(lower), ("thick", "wide")) / (NX * NY)
    return (phase, density, flux)


def solution(mesh):
    in_specs = (P("thick", "wide", None), P("thick", "wide", None))
    out_specs = (P("thick", "wide", None), P("thick", "wide", None), P())
    return jax.shard_map(
        per_device, mesh=mesh, in_specs=in_specs, out_specs=out_specs, check_vma=False
    )
```

profile of v0, /device:TPU:12, one launch (start us, length us, event | category | flops | bytes accessed | tf_op | source)
XLA Modules:
  0.0 1466.6 jit_solution(4611788430884908214)
XLA Ops:
  5.6 32.7 %fusion.1 = f32[2,32,64,512]{3,2,1,0:T(8,128)} fusion(f32[1,32,64,512]{3,2,1,0:T(8,128)S(1)} %fusion.5, f32[1,32,64,512]{3,2,1,0:T(8,128)S(1)} %bitcast.208), kind=kOutput, calls=%fused_computation.12 | convolution fusion | flops 12890669056 | bytes 16777216 | tf_op jit(solution)/shard_map/fzxy,yk->fzxk/dot_general | solution.py:43
  38.3 16.3 %copy.13 = f32[2,32,64,512]{2,1,0,3:T(8,128)} copy(f32[2,32,64,512]{3,2,1,0:T(8,128)} %fusion.1) | data formatting | bytes 16777216 | tf_op jit(solution)/shard_map/fzxy,yk->fzxk/dot_general | solution.py:43
  54.6 15.4 %reshape.91 = f32[8,1,262144]{2,1,0:T(1,128)} reshape(f32[512,2,32,64]{3,2,1,0:T(8,128)} %bitcast.189) | data formatting | bytes 16777216
  76.5 25.5 %fusion.63 = f32[2,32,64,512]{3,2,1,0:T(8,128)} fusion(f32[1,32,64,512]{3,2,1,0:T(8,128)} %copy-done.5, f32[1,32,64,512]{3,2,1,0:T(8,128)} %bitcast.207), kind=kOutput, calls=%fused_computation.115 | convolution fusion | flops 12892766208 | bytes 16777216 | tf_op jit(solution)/shard_map/fzxy,yk->fzxk/dot_general | solution.py:43
  102.0 16.8 %copy.15 = f32[2,32,64,512]{2,1,0,3:T(8,128)} copy(f32[2,32,64,512]{3,2,1,0:T(8,128)} %fusion.63) | data formatting | bytes 16777216 | tf_op jit(solution)/shard_map/neg | solution.py:93
  118.8 15.5 %reshape.93 = f32[8,1,262144]{2,1,0:T(1,128)} reshape(f32[512,2,32,64]{3,2,1,0:T(8,128)} %bitcast.190) | data formatting | bytes 16777216
  134.3 122.8 %all-to-all-done = f32[8,1,262144]{2,1,0:T(1,128)} async-done(((f32[8,1,262144]{2,1,0:T(1,128)}), f32[8,1,262144]{2,1,0:T(1,128)}, u32[]{:S(2)}, u32[]{:S(2)}) %all-to-all-start) | async-done | bytes 8388640 | tf_op jit(solution)/shard_map/all_to_all | solution.py:95
  265.0 26.3 %reduce = f32[8,262144]{1,0:T(8,128)} reduce(f32[8,1,262144]{2,1,0:T(1,128)} %all-to-all-done, f32[]{:T(128)} %broadcast.342), dimensions={1}, to_apply=%all_to_all.104.reduce_sub_computation | reduce | bytes 16777220 | tf_op jit(solution)/shard_map/all_to_all | solution.py:95
  291.2 15.6 %reshape.92 = f32[512,2,32,64]{3,2,1,0:T(8,128)} reshape(f32[8,262144]{1,0:T(8,128)} %reduce) | data formatting | bytes 16777216
  306.9 17.8 %copy.40 = f32[2,32,64,8,64]{2,3,4,1,0:T(8,128)} copy(f32[2,32,64,8,64]{2,1,0,4,3:T(8,128)} %bitcast.195) | data formatting | bytes 16777216 | tf_op jit(solution)/shard_map/all_to_all | solution.py:95
  324.7 14.2 all_to_all.107
  338.9 25.5 %fusion.75 = f32[2,32,64,512]{3,2,1,0:T(8,128)} fusion(f32[2,32,512,64]{2,3,1,0:T(8,128)} %all_to_all.107), kind=kOutput, calls=%fused_computation.133 | convolution fusion | flops 12888571904 | bytes 16777216 | tf_op jit(solution)/shard_map/fzxy,xk->fzyk/dot_general | solution.py:43
  364.5 79.8 %all-to-all-done.1 = f32[8,1,262144]{2,1,0:T(1,128)} async-done(((f32[8,1,262144]{2,1,0:T(1,128)}), f32[8,1,262144]{2,1,0:T(1,128)}, u32[]{:S(2)}, u32[]{:S(2)}) %all-to-all-start.1) | async-done | bytes 8388640 | tf_op jit(solution)/shard_map/all_to_all | solution.py:96
  444.3 26.5 %reduce.1 = f32[8,262144]{1,0:T(8,128)} reduce(f32[8,1,262144]{2,1,0:T(1,128)} %all-to-all-done.1, f32[]{:T(128)} %broadcast.342), dimensions={1}, to_apply=%all_to_all.108.reduce_sub_computation | reduce | bytes 16777220 | tf_op jit(solution)/shard_map/all_to_all | solution.py:96
  470.8 15.6 %reshape.94 = f32[512,2,32,64]{3,2,1,0:T(8,128)} reshape(f32[8,262144]{1,0:T(8,128)} %reduce.1) | data formatting | bytes 16777216
  486.4 17.8 %copy.39 = f32[2,32,64,8,64]{2,3,4,1,0:T(8,128)} copy(f32[2,32,64,8,64]{2,1,0,4,3:T(8,128)} %bitcast.197) | data formatting | bytes 16777216 | tf_op jit(solution)/shard_map/all_to_all | solution.py:96
  504.2 14.7 %all_to_all.111 = f32[2,32,512,64]{2,3,1,0:T(8,128)} reshape(f32[2,32,8,64,64]{3,2,4,1,0:T(8,128)} %bitcast.198) | data formatting | bytes 16777216 | tf_op jit(solution)/shard_map/all_to_all | solution.py:96
  518.9 26.8 %convolution_add_fusion = f32[2,32,64,512]{3,2,1,0:T(8,128)} fusion(f32[2,32,64,512]{3,2,1,0:T(8,128)} %fusion.75, f32[2,32,512,64]{2,3,1,0:T(8,128)} %all_to_all.111), kind=kOutput, calls=%fused_computation.117 | convolution fusion | flops 12890669056 | bytes 25165824 | tf_op jit(solution)/shard_map/fzxy,xk->fzyk/dot_general | solution.py:43
  545.6 16.4 %copy.17 = f32[2,32,64,512]{2,1,0,3:T(8,128)} copy(f32[2,32,64,512]{3,2,1,0:T(8,128)} %convolution_add_fusion) | data formatting | bytes 16777216 | tf_op jit(solution)/shard_map/add | solution.py:100
  562.1 14.3 reshape.95
  582.5 24.2 %fusion.73 = f32[2,32,64,512]{3,2,1,0:T(8,128)S(1)} fusion(f32[2,32,512,64]{2,3,1,0:T(8,128)} %all_to_all.111), kind=kOutput, calls=%fused_computation.131 | convolution fusion | flops 12888571904 | bytes 16777216 | tf_op jit(solution)/shard_map/fzxy,xk->fzyk/dot_general | solution.py:43
  606.8 25.9 %convolution_subtract_fusion = f32[2,32,64,512]{3,2,1,0:T(8,128)} fusion(f32[2,32,64,512]{3,2,1,0:T(8,128)S(1)} %fusion.73, f32[2,32,512,64]{2,3,1,0:T(8,128)} %all_to_all.107), kind=kOutput, calls=%fused_computation.116 | convolution fusion | flops 12890669056 | bytes 25165824 | tf_op jit(solution)/shard_map/fzxy,xk->fzyk/dot_general | solution.py:43
  632.6 16.3 %copy.19 = f32[2,32,64,512]{2,1,0,3:T(8,128)} copy(f32[2,32,64,512]{3,2,1,0:T(8,128)} %convolution_subtract_fusion) | data formatting | bytes 16777216 | tf_op jit(solution)/shard_map/sub | solution.py:101
  648.9 14.4 reshape.97
  663.3 10.8 all-to-all-done.2
  681.7 28.3 %reduce.2 = f32[4,524288]{1,0:T(4,128)} reduce(f32[4,1,524288]{2,1,0:T(1,128)} %all-to-all-done.2, f32[]{:T(128)} %broadcast.342), dimensions={1}, to_apply=%all_to_all.112.reduce_sub_computation | reduce | bytes 16777220 | tf_op jit(solution)/shard_map/all_to_all | solution.py:103
  709.9 16.8 %reshape.96 = f32[512,2,32,64]{3,2,1,0:T(8,128)} reshape(f32[4,524288]{1,0:T(4,128)} %reduce.2) | data formatting | bytes 16777216
  726.7 15.9 %copy.18 = f32[2,32,64,4,128]{4,1,3,2,0:T(8,128)} copy(f32[2,32,64,4,128]{2,1,0,4,3:T(8,128)} %bitcast.193) | data formatting | bytes 16777216 | tf_op jit(solution)/shard_map/all_to_all | solution.py:103
  742.7 12.2 fusion.108
  754.8 18.2 %all-to-all-done.3 = f32[4,1,524288]{2,1,0:T(1,128)} async-done(((f32[4,1,524288]{2,1,0:T(1,128)}), f32[4,1,524288]{2,1,0:T(1,128)}, u32[]{:S(2)}, u32[]{:S(2)}) %all-to-all-start.3) | async-done | bytes 8388640 | tf_op jit(solution)/shard_map/all_to_all | solution.py:104
  773.1 28.6 %reduce.3 = f32[4,524288]{1,0:T(4,128)} reduce(f32[4,1,524288]{2,1,0:T(1,128)} %all-to-all-done.3, f32[]{:T(128)} %broadcast.342), dimensions={1}, to_apply=%all_to_all.116.reduce_sub_computation | reduce | bytes 16777220 | tf_op jit(solution)/shard_map/all_to_all | solution.py:104
  801.7 16.8 %reshape.98 = f32[512,2,32,64]{3,2,1,0:T(8,128)} reshape(f32[4,524288]{1,0:T(4,128)} %reduce.3) | data formatting | bytes 16777216
  818.5 15.8 %copy.20 = f32[2,32,64,4,128]{4,1,3,2,0:T(8,128)} copy(f32[2,32,64,4,128]{2,1,0,4,3:T(8,128)} %bitcast.194) | data formatting | bytes 16777216 | tf_op jit(solution)/shard_map/all_to_all | solution.py:104
  834.3 11.3 fusion.106
  845.6 12.3 add_bitcast_fusion
  858.0 10.2 subtract_bitcast_fusion
  891.6 8.6 fusion.112
  900.2 8.6 add_bitcast_fusion.2
  913.3 24.9 %all-to-all-done.4 = f32[64,128,128]{2,0,1:T(8,128)} async-done(((f32[64,128,128]{2,0,1:T(8,128)}), f32[64,128,128]{2,0,1:T(8,128)}, u32[]{:S(2)}, u32[]{:S(2)}) %all-to-all-start.4) | async-done | bytes 4194336 | tf_op jit(solution)/shard_map/all_to_all | solution.py:117
  944.9 7.8 copy.44
  958.1 14.3 fusion.82
  972.5 19.0 %all-to-all-done.5 = f32[64,128,128]{2,0,1:T(8,128)} async-done(((f32[64,128,128]{2,0,1:T(8,128)}), f32[64,128,128]{2,0,1:T(8,128)}, u32[]{:S(2)}, u32[]{:S(2)}) %all-to-all-start.5) | async-done | bytes 4194336 | tf_op jit(solution)/shard_map/all_to_all | solution.py:118
  991.5 7.8 copy.43
  1004.7 14.9 %subtract_bitcast_fusion.1 = f32[32,512,64]{1,2,0:T(8,128)} fusion(f32[512,64,32]{0,1,2:T(8,128)} %fusion.82, f32[64,32,512]{2,0,1:T(8,128)} %all_to_all.127), kind=kOutput, calls=%fused_computation.112 | convolution fusion | flops 6447169536 | bytes 12582912 | tf_op jit(solution)/shard_map/yzk,kx->zxy/dot_general | solution.py:43
  1019.6 9.2 copy.25
  1028.8 9.8 reshape.99
  1046.0 12.6 fusion.78
  1058.7 12.4 add_bitcast_fusion.1
  1071.0 9.2 copy.27
  1080.2 9.9 reshape.101
  1090.1 46.9 %all-to-all-done.6 = f32[8,1,131072]{2,1,0:T(1,128)} async-done(((f32[8,1,131072]{2,1,0:T(1,128)}), f32[8,1,131072]{2,1,0:T(1,128)}, u32[]{:S(2)}, u32[]{:S(2)}) %all-to-all-start.6) | async-done | bytes 4194336 | tf_op jit(solution)/shard_map/all_to_all | solution.py:123
  1150.1 14.0 reduce.4
  1164.1 8.7 reshape.100
  1172.8 11.6 copy.42
  1191.8 14.5 fusion.80
  1206.3 28.0 %all-to-all-done.7 = f32[8,1,131072]{2,1,0:T(1,128)} async-done(((f32[8,1,131072]{2,1,0:T(1,128)}), f32[8,1,131072]{2,1,0:T(1,128)}, u32[]{:S(2)}, u32[]{:S(2)}) %all-to-all-start.7) | async-done | bytes 4194336 | tf_op jit(solution)/shard_map/all_to_all | solution.py:124
  1234.3 14.2 reduce.5
  1248.5 8.8 reshape.102
  1257.3 11.5 copy.41
  1276.3 24.5 %multiply_add_fusion = (f32[32,64,512]{2,1,0:T(8,128)S(1)}, f32[32,64,512]{2,1,0:T(8,128)}) fusion(f32[32,64,512]{2,1,0:T(8,128)} %fusion.80, f32[32,64,512]{2,1,0:T(8,128)} %all_to_all.135), kind=kOutput, calls=%fused_computation.110 | convolution fusion | flops 6453460992 | bytes 16777216 | tf_op jit(solution)/shard_map/zxk,ky->zxy/dot_general | solution.py:43
  1334.5 16.4 %fusion.39 = (f32[32,64,512]{2,1,0:T(8,128)}, f32[32,64,512]{2,1,0:T(8,128)}, f32[32,64,512]{2,1,0:T(8,128)}, f32[32,64,512]{2,1,0:T(8,128)}) fusion(f32[34,66,512]{2,1,0:T(8,128)S(1)} %get-tuple-element.44, f32[32,64,511]{2,1,0:T(8,128)} %get-tuple-element.49, f32[32,64,1]{2,1,0:T(8,128)} %get-tuple-element.47, f32[32,64,1]{2,1,0:T(8,128)} %get-tuple-element.48, ...), kind=kLoop, calls=%fused_computation.65 | loop fusion | flops 36700160 | bytes 75497472 | tf_op jit(solution)/shard_map/add | solution.py:65
  1377.6 10.6 fusion.28
  1409.9 11.6 fusion.224
  1421.5 42.8 %psum.7 = f32[]{:T(128)} all-reduce(f32[]{:T(128)} %get-tuple-element.7), channel_id=1, replica_groups=mesh['thick'=4,'wide'=8] {'thick','wide'}, use_global_device_ids=true, to_apply=%region_1.2 | all-reduce | flops 1 | bytes 8 | tf_op jit(solution)/shard_map/psum | solution.py:149
  (108 shorter events, 195.9 us)
Async XLA Ops:
  0.6 4.9 copy-start.4
  3.5 2.0 copy-start.5
  70.0 187.1 %all-to-all-start = ((f32[8,1,262144]{2,1,0:T(1,128)}), f32[8,1,262144]{2,1,0:T(1,128)}, u32[]{:S(2)}, u32[]{:S(2)}) async-start(f32[8,1,262144]{2,1,0:T(1,128)} %reshape.91), calls=%async_computation | async-start | bytes 16777216 | tf_op jit(solution)/shard_map/all_to_all | solution.py:95
  257.1 187.2 %all-to-all-start.1 = ((f32[8,1,262144]{2,1,0:T(1,128)}), f32[8,1,262144]{2,1,0:T(1,128)}, u32[]{:S(2)}, u32[]{:S(2)}) async-start(f32[8,1,262144]{2,1,0:T(1,128)} %reshape.93), calls=%async_computation.1 | async-start | bytes 16777216 | tf_op jit(solution)/shard_map/all_to_all | solution.py:96
  576.4 97.7 %all-to-all-start.2 = ((f32[4,1,524288]{2,1,0:T(1,128)}), f32[4,1,524288]{2,1,0:T(1,128)}, u32[]{:S(2)}, u32[]{:S(2)}) async-start(f32[4,1,524288]{2,1,0:T(1,128)} %reshape.95), calls=%async_computation.2 | async-start | bytes 16777216 | tf_op jit(solution)/shard_map/all_to_all | solution.py:103
  674.1 99.0 %all-to-all-start.3 = ((f32[4,1,524288]{2,1,0:T(1,128)}), f32[4,1,524288]{2,1,0:T(1,128)}, u32[]{:S(2)}, u32[]{:S(2)}) async-start(f32[4,1,524288]{2,1,0:T(1,128)} %reshape.97), calls=%async_computation.3 | async-start | bytes 16777216 | tf_op jit(solution)/shard_map/all_to_all | solution.py:104
  834.3 11.3 copy-start
  834.3 23.7 %slice-start = ((s8[8388608]{0:T(1024)(128)(4,1)}), s8[4194304]{0:T(1024)(128)(4,1)S(1)}, s32[]{:S(2)}) async-start(s8[8388608]{0:T(1024)(128)(4,1)} %bitcast.184), calls=%async_computation.8 | async-start | bytes 8388608
  845.6 12.4 slice-start.1
  858.0 10.2 copy-start.6
  868.2 5.8 copy-start.7
  885.1 53.1 %all-to-all-start.4 = ((f32[64,128,128]{2,0,1:T(8,128)}), f32[64,128,128]{2,0,1:T(8,128)}, u32[]{:S(2)}, u32[]{:S(2)}) async-start(f32[64,128,128]{2,0,1:T(8,128)} %copy.21), calls=%async_computation.4 | async-start | bytes 8388608 | tf_op jit(solution)/shard_map/all_to_all | solution.py:117
  938.2 53.3 %all-to-all-start.5 = ((f32[64,128,128]{2,0,1:T(8,128)}), f32[64,128,128]{2,0,1:T(8,128)}, u32[]{:S(2)}, u32[]{:S(2)}) async-start(f32[64,128,128]{2,0,1:T(8,128)} %copy.23), calls=%async_computation.5 | async-start | bytes 8388608 | tf_op jit(solution)/shard_map/all_to_all | solution.py:118
  1038.6 98.4 %all-to-all-start.6 = ((f32[8,1,131072]{2,1,0:T(1,128)}), f32[8,1,131072]{2,1,0:T(1,128)}, u32[]{:S(2)}, u32[]{:S(2)}) async-start(f32[8,1,131072]{2,1,0:T(1,128)} %reshape.99), calls=%async_computation.6 | async-start | bytes 8388608 | tf_op jit(solution)/shard_map/all_to_all | solution.py:123
  1046.0 12.7 copy-start.1
  1137.0 97.2 %all-to-all-start.7 = ((f32[8,1,131072]{2,1,0:T(1,128)}), f32[8,1,131072]{2,1,0:T(1,128)}, u32[]{:S(2)}, u32[]{:S(2)}) async-start(f32[8,1,131072]{2,1,0:T(1,128)} %reshape.101), calls=%async_computation.7 | async-start | bytes 8388608 | tf_op jit(solution)/shard_map/all_to_all | solution.py:124
  1145.0 4.4 collective-permute-start
  1145.1 157.1 %collective-permute-start.1 = (f32[1,64,512]{2,1,0:T(8,128)S(1)}, f32[1,64,512]{2,1,0:T(8,128)S(1)}, u32[]{:S(2)}, u32[]{:S(2)}) collective-permute-start(f32[1,64,512]{2,1,0:T(8,128)S(1)} %get-tuple-element.41), channel_id=1, source_target_pairs={{8,0},{16,8},{24,16},{0,24},{9,1},{17,9},{25,17},{1,25},{10,2},{18... | collective-permute-start | bytes 393224 | tf_op jit(solution)/shard_map/ppermute | solution.py:25
  1268.7 32.9 %slice-start.2 = ((s8[4456448]{0:T(1024)(128)(4,1)}), s8[262144]{0:T(1024)(128)(4,1)S(1)}, s32[]{:S(2)}) async-start(s8[4456448]{0:T(1024)(128)(4,1)} %bitcast.209), calls=%async_computation.10 | async-start | bytes 524288
  1276.2 25.4 %slice-start.3 = ((s8[4456448]{0:T(1024)(128)(4,1)}), s8[4194304]{0:T(1024)(128)(4,1)S(1)}, s32[]{:S(2)}) async-start(s8[4456448]{0:T(1024)(128)(4,1)} %bitcast.209), calls=%async_computation.11 | async-start | bytes 8388608
  1276.3 25.4 %copy-start.9 = (f32[32,64,512]{2,1,0:T(8,128)S(1)}, f32[32,64,512]{2,1,0:T(8,128)}, u32[]{:S(2)}) copy-start(f32[32,64,512]{2,1,0:T(8,128)} %param.3) | copy-start | bytes 12582916
  1300.7 4.6 collective-permute-start.5
  1301.7 5.1 collective-permute-start.4
  1302.2 14.2 copy-start.8
  1306.9 6.2 collective-permute-start.7
  1310.0 5.3 collective-permute-start.6
  1310.2 6.3 collective-permute-start.3
  1313.1 5.2 collective-permute-start.2
  1350.9 17.4 %copy-start.2 = (f32[32,64,512]{2,1,0:T(8,128)S(1)}, f32[32,64,512]{2,1,0:T(8,128)}, u32[]{:S(2)}) copy-start(f32[32,64,512]{2,1,0:T(8,128)} %get-tuple-element.3) | copy-start | bytes 12582916
  1352.1 3.7 collective-permute-start.9
  1352.1 5.1 collective-permute-start.8
  1358.6 4.7 collective-permute-start.11
  1361.3 7.0 collective-permute-start.10
  1388.2 3.7 collective-permute-start.13
  1388.3 5.1 collective-permute-start.12
  1393.5 4.4 collective-permute-start.15
  1395.5 5.2 collective-permute-start.14
  1404.7 5.2 copy-start.3
where the time goes:
time: 1480 us; the launch traced here: 1470 us
  local copies, waits for them, and re-layouts  443 us (30%)
  waiting for transfers between devices  383 us (26%)
  matrix products  329 us (22%)
  other arithmetic  196 us (13%)
  starting transfers between devices  69.8 us (5%)
  blocking collectives  42.8 us (3%)
    dot_general x20, matrix products, product(): return jnp.einsum(form, left, right, precision=lax.Precision.HIGHEST)  329 us
    unnamed x42, local copies, waits for them, and re-layouts  165 us
    all_to_all x1, waiting for transfers between devices, per_device(): lax.all_to_all(real_part, 'wide', split_axis=3, concat_axis=2, tiled=True)  123 us
    all_to_all x1, waiting for transfers between devices, per_device(): lax.all_to_all(imag_part, 'wide', split_axis=3, concat_axis=2, tiled=True)  79.8 us
    all_to_all x1, waiting for transfers between devices, per_device(): lax.all_to_all(pair[0], 'wide', split_axis=1, concat_axis=2, tiled=True)  46.9 us
    psum x1, blocking collectives, per_device(): flux = lax.psum(jnp.sum(lower), ('thick', 'wide')) / (NX * NY)  42.8 us
    all_to_all x3, local copies, waits for them, and re-layouts, per_device(): lax.all_to_all(real_part, 'wide', split_axis=3, concat_axis=2, tiled=True)  32.6 us
    all_to_all x2, local copies, waits for them, and re-layouts, per_device(): lax.all_to_all(imag_part, 'wide', split_axis=3, concat_axis=2, tiled=True)  32.5 us
  transfers between devices with their start and end apart: 24, of which 21 were waited for; matrix products, arithmetic and copies ran while one was open for 34% of the time, Pallas kernels for 0%

commit v1 on v0

--- a/solution.py
+++ b/solution.py
@@ -12,6 +12,28 @@
 stabilizer = 3.0
 gradient_energy = 2.0
 walk_step = 0.16
+
+
+def cut_along(x, dim, size):
+    before, after = (x.shape[:dim], x.shape[dim + 1 :])
+    return jnp.moveaxis(x.reshape(*before, size, -1, *after), dim, 0)
+
+
+def laid_out(blocks, dim):
+    blocks = jnp.moveaxis(blocks, 0, dim)
+    dims = blocks.shape
+    return blocks.reshape(*dims[:dim], dims[dim] * dims[dim + 1], *dims[dim + 2 :])
+
+
+def exchange_directly(x, axis, split_dim, concat_dim):
+    size, place = (lax.axis_size(axis), lax.axis_index(axis))
+    tiles = cut_along(x, split_dim, size)
+    outs = [tiles[place]]
+    for step in range(1, size):
+        sent = tiles[(place + step) % size]
+        outs.append(lax.ppermute(sent, axis, [(i, (i + step) % size) for i in range(size)]))
+    tiles = jnp.stack(outs)[(place - jnp.arange(size)) % size]
+    return laid_out(tiles, concat_dim)
 
 
 def with_halo(array, sides, width):
@@ -93,7 +115,7 @@
     imag_part = -product(form, fields, sine_y)
     pair = (
         lax.all_to_all(real_part, "wide", split_axis=3, concat_axis=2, tiled=True),
-        lax.all_to_all(imag_part, "wide", split_axis=3, concat_axis=2, tiled=True),
+        exchange_directly(imag_part, "wide", 3, 2),
     )
     forward_real_part, forward_imag_part = pair
     form = "fzxy,xk->fzyk"

time: 1480 us -> 1730 us (1.17)
  waiting for transfers between devices: 383 us -> 603 us
  local copies, waits for them, and re-layouts: 443 us -> 494 us
  other arithmetic: 196 us -> 168 us
    ppermute x0 -> x7, waiting for transfers between devices: none -> 419 us  [exchange_directly(): lax.ppermute(sent, axis, [(i, (i + step) % size) for i in range(size)])]
    all_to_all x1, waiting for transfers between devices: 123 us -> 0.01 us  [per_device(): lax.all_to_all(real_part, 'wide', split_axis=3, concat_axis=2, tiled=True)]
    all_to_all x1 -> x0, waiting for transfers between devices: 79.8 us -> none  [per_device(): lax.all_to_all(imag_part, 'wide', split_axis=3, concat_axis=2, tiled=True)]
    another operation x0 -> x2, local copies, waits for them, and re-layouts: none -> 60.5 us
    all_to_all x2 -> x0, local copies, waits for them, and re-layouts: 32.5 us -> none  [per_device(): lax.all_to_all(imag_part, 'wide', split_axis=3, concat_axis=2, tiled=True)]
    reshape x0 -> x2, local copies, waits for them, and re-layouts: none -> 27.1 us  [the longest x1 14.2 us: laid_out(): blocks.reshape(*dims[:dim], dims[dim] * dims[dim + 1], *dims[dim + 2:])]
    all_to_all x1 -> x0, other arithmetic: 26.5 us -> none  [per_device(): lax.all_to_all(imag_part, 'wide', split_axis=3, concat_axis=2, tiled=True)]
    all_to_all x1, waiting for transfers between devices: 28 us -> 46.7 us  [per_device(): lax.all_to_all(pair[1], 'wide', split_axis=1, concat_axis=2, tiled=True)]
  transfers between devices with their start and end apart: 24 -> 30, of which waited for: 21 -> 26; matrix products, arithmetic and copies ran while one was open for 34% -> 31% of each run, Pallas kernels for 0% -> 0%
where the time goes in v1:
time: 1730 us; the launch traced here: 1720 us
  waiting for transfers between devices  603 us (35%)
  local copies, waits for them, and re-layouts  494 us (29%)
  matrix products  326 us (19%)
  other arithmetic  168 us (10%)
  starting transfers between devices  83.2 us (5%)
  blocking collectives  46.5 us (3%)
    ppermute x7, waiting for transfers between devices, exchange_directly(): lax.ppermute(sent, axis, [(i, (i + step) % size) for i in range(size)])  419 us
    dot_general x20, matrix products, product(): return jnp.einsum(form, left, right, precision=lax.Precision.HIGHEST)  326 us
    unnamed x51, local copies, waits for them, and re-layouts  146 us
    another operation x1, local copies, waits for them, and re-layouts  59.1 us
    all_to_all x1, waiting for transfers between devices, per_device(): lax.all_to_all(pair[1], 'wide', split_axis=1, concat_axis=2, tiled=True)  46.7 us
    psum x1, blocking collectives, per_device(): flux = lax.psum(jnp.sum(lower), ('thick', 'wide')) / (NX * NY)  46.5 us
    all_to_all x1, waiting for transfers between devices, per_device(): lax.all_to_all(pair[0], 'wide', split_axis=1, concat_axis=2, tiled=True)  42.1 us
  transfers between devices with their start and end apart: 30, of which 26 were waited for; matrix products, arithmetic and copies ran while one was open for 31% of the time, Pallas kernels for 0%

profile of v1, /device:TPU:12, one launch (start us, length us, event | category | flops | bytes accessed | tf_op | source)
XLA Modules:
  0.0 1724.4 jit_solution(11380762123890232220)
XLA Ops:
  5.6 32.8 %fusion.1 = f32[2,32,64,512]{3,2,1,0:T(8,128)} fusion(f32[1,32,64,512]{3,2,1,0:T(8,128)S(1)} %fusion.5, f32[1,32,64,512]{3,2,1,0:T(8,128)S(1)} %bitcast.227), kind=kOutput, calls=%fused_computation.12 | convolution fusion | flops 12890669056 | bytes 16777216 | tf_op jit(solution)/shard_map/fzxy,yk->fzxk/dot_general | solution.py:65
  38.3 16.3 copy.27
  54.6 15.4 reshape.171
  76.9 25.6 %fusion.63 = f32[2,32,64,512]{3,2,1,0:T(8,128)} fusion(f32[1,32,64,512]{3,2,1,0:T(8,128)} %copy-done.5, f32[1,32,64,512]{3,2,1,0:T(8,128)} %bitcast.226), kind=kOutput, calls=%fused_computation.115 | convolution fusion | flops 12892766208 | bytes 16777216 | tf_op jit(solution)/shard_map/fzxy,yk->fzxk/dot_general | solution.py:65
  102.5 12.9 reshape.153
  115.4 59.1 %constant_dynamic-slice_fusion = (f32[2,32,64,1,64]{4,3,2,1,0:T(1,128)}, f32[2,32,64,1,64]{4,3,2,1,0:T(1,128)}, f32[2,32,64,1,64]{4,3,2,1,0:T(1,128)}, f32[2,32,...) fusion(f32[2,32,64,8,64]{4,3,2,1,0:T(8,128)} %reshape.153, ...), kind=kLoop, calls=%fused_computation.218 | loop fusion | bytes 16777248 | tf_op jit(solution)/shard_map/dynamic-slice.7
  184.3 76.1 %collective-permute-done = f32[2,32,64,64]{3,2,1,0:T(8,128)S(1)} collective-permute-done((f32[2,32,64,64]{3,2,1,0:T(8,128)}, f32[2,32,64,64]{3,2,1,0:T(8,128)S(1)}, u32[]{:S(2)}, u32[]{:S(2)}) %collective-permute-start) | collective-permute-done | bytes 1048608 | tf_op jit(solution)/shard_map/ppermute | solution.py:34
  264.8 38.6 %collective-permute-done.1 = f32[2,32,64,64]{3,2,1,0:T(8,128)S(1)} collective-permute-done((f32[2,32,64,64]{3,2,1,0:T(8,128)}, f32[2,32,64,64]{3,2,1,0:T(8,128)S(1)}, u32[]{:S(2)}, u32[]{:S(2)}) %collective-permute-start.1) | collective-permute-done | bytes 1048608 | tf_op jit(solution)/shard_map/ppermute | solution.py:34
  309.7 217.4 %collective-permute-done.2 = f32[2,32,64,64]{3,2,1,0:T(8,128)S(1)} collective-permute-done((f32[2,32,64,64]{3,2,1,0:T(8,128)}, f32[2,32,64,64]{3,2,1,0:T(8,128)S(1)}, u32[]{:S(2)}, u32[]{:S(2)}) %collective-permute-start.2) | collective-permute-done | bytes 1048608 | tf_op jit(solution)/shard_map/ppermute | solution.py:34
  528.7 43.4 %collective-permute-done.3 = f32[2,32,64,64]{3,2,1,0:T(8,128)S(1)} collective-permute-done((f32[2,32,64,64]{3,2,1,0:T(8,128)}, f32[2,32,64,64]{3,2,1,0:T(8,128)S(1)}, u32[]{:S(2)}, u32[]{:S(2)}) %collective-permute-start.3) | collective-permute-done | bytes 1048608 | tf_op jit(solution)/shard_map/ppermute | solution.py:34
  573.6 43.4 %collective-permute-done.4 = f32[2,32,64,64]{3,2,1,0:T(8,128)S(1)} collective-permute-done((f32[2,32,64,64]{3,2,1,0:T(8,128)}, f32[2,32,64,64]{3,2,1,0:T(8,128)S(1)}, u32[]{:S(2)}, u32[]{:S(2)}) %collective-permute-start.4) | collective-permute-done | bytes 1048608 | tf_op jit(solution)/shard_map/ppermute | solution.py:34
  621.4 13.8 gather_fusion
  635.2 17.5 %copy.29 = f32[2,32,8,64,64]{3,2,4,1,0:T(8,128)} copy(f32[2,32,8,64,64]{4,3,1,0,2:T(8,128)} %bitcast.215) | data formatting | bytes 16777216 | tf_op jit(solution)/shard_map/transpose | solution.py:23
  652.7 14.2 reshape.154
  666.9 25.7 %fusion.73 = f32[2,32,64,512]{3,2,1,0:T(8,128)} fusion(f32[2,32,512,64]{2,3,1,0:T(8,128)} %reshape.154), kind=kOutput, calls=%fused_computation.138 | convolution fusion | flops 12888571904 | bytes 16777216 | tf_op jit(solution)/shard_map/fzxy,xk->fzyk/dot_general | solution.py:65
  693.0 26.7 %reduce = f32[8,262144]{1,0:T(8,128)} reduce(f32[8,1,262144]{2,1,0:T(1,128)} %all-to-all-done, f32[]{:T(128)} %broadcast.418), dimensions={1}, to_apply=%all_to_all.91.reduce_sub_computation | reduce | bytes 16777220 | tf_op jit(solution)/shard_map/all_to_all | solution.py:117
  719.8 15.7 reshape.172
  735.4 17.8 %copy.51 = f32[2,32,64,8,64]{2,3,4,1,0:T(8,128)} copy(f32[2,32,64,8,64]{2,1,0,4,3:T(8,128)} %bitcast.216) | data formatting | bytes 16777216 | tf_op jit(solution)/shard_map/all_to_all | solution.py:117
  753.2 14.3 all_to_all.94
  767.6 26.9 %convolution_subtract_fusion = f32[2,32,64,512]{3,2,1,0:T(8,128)} fusion(f32[2,32,64,512]{3,2,1,0:T(8,128)} %fusion.73, f32[2,32,512,64]{2,3,1,0:T(8,128)} %all_to_all.94), kind=kOutput, calls=%fused_computation.116 | convolution fusion | flops 12890669056 | bytes 25165824 | tf_op jit(solution)/shard_map/fzxy,xk->fzyk/dot_general | solution.py:65
  794.4 16.7 copy.32
  811.1 14.4 reshape.175
  831.6 24.2 %fusion.75 = f32[2,32,64,512]{3,2,1,0:T(8,128)S(1)} fusion(f32[2,32,512,64]{2,3,1,0:T(8,128)} %all_to_all.94), kind=kOutput, calls=%fused_computation.140 | convolution fusion | flops 12888571904 | bytes 16777216 | tf_op jit(solution)/shard_map/fzxy,xk->fzyk/dot_general | solution.py:65
  855.8 25.8 %convolution_add_fusion = f32[2,32,64,512]{3,2,1,0:T(8,128)} fusion(f32[2,32,64,512]{3,2,1,0:T(8,128)S(1)} %fusion.75, f32[2,32,512,64]{2,3,1,0:T(8,128)} %reshape.154), kind=kOutput, calls=%fused_computation.117 | convolution fusion | flops 12890669056 | bytes 25165824 | tf_op jit(solution)/shard_map/fzxy,xk->fzyk/dot_general | solution.py:65
  881.6 16.3 copy.30
  897.9 14.3 reshape.173
  912.2 10.9 all-to-all-done.2
  930.7 28.3 %reduce.2 = f32[4,524288]{1,0:T(4,128)} reduce(f32[4,1,524288]{2,1,0:T(1,128)} %all-to-all-done.2, f32[]{:T(128)} %broadcast.418), dimensions={1}, to_apply=%all_to_all.99.reduce_sub_computation | reduce | bytes 16777220 | tf_op jit(solution)/shard_map/all_to_all | solution.py:126
  959.0 16.8 reshape.176
  975.9 16.2 copy.33
  992.1 12.1 fusion.106
  1004.2 18.0 %all-to-all-done.1 = f32[4,1,524288]{2,1,0:T(1,128)} async-done(((f32[4,1,524288]{2,1,0:T(1,128)}), f32[4,1,524288]{2,1,0:T(1,128)}, u32[]{:S(2)}, u32[]{:S(2)}) %all-to-all-start.1) | async-done | bytes 8388640 | tf_op jit(solution)/shard_map/all_to_all | solution.py:125
  1022.1 28.4 %reduce.1 = f32[4,524288]{1,0:T(4,128)} reduce(f32[4,1,524288]{2,1,0:T(1,128)} %all-to-all-done.1, f32[]{:T(128)} %broadcast.418), dimensions={1}, to_apply=%all_to_all.95.reduce_sub_computation | reduce | bytes 16777220 | tf_op jit(solution)/shard_map/all_to_all | solution.py:125
  1050.6 16.8 reshape.174
  1067.4 15.7 copy.31
  1083.2 11.3 fusion.108
  1094.5 12.3 subtract_bitcast_fusion
  1106.8 10.4 add_bitcast_fusion
  1140.3 8.6 fusion.114
  1148.9 8.6 subtract_bitcast_fusion.2
  1162.0 24.9 %all-to-all-done.4 = f32[64,128,128]{2,0,1:T(8,128)} async-done(((f32[64,128,128]{2,0,1:T(8,128)}), f32[64,128,128]{2,0,1:T(8,128)}, u32[]{:S(2)}, u32[]{:S(2)}) %all-to-all-start.4) | async-done | bytes 4194336 | tf_op jit(solution)/shard_map/all_to_all | solution.py:140
  1207.0 14.6 fusion.78
  1221.7 18.6 %all-to-all-done.3 = f32[64,128,128]{2,0,1:T(8,128)} async-done(((f32[64,128,128]{2,0,1:T(8,128)}), f32[64,128,128]{2,0,1:T(8,128)}, u32[]{:S(2)}, u32[]{:S(2)}) %all-to-all-start.3) | async-done | bytes 4194336 | tf_op jit(solution)/shard_map/all_to_all | solution.py:139
  1253.5 14.9 add_bitcast_fusion.1
  1268.4 9.2 copy.40
  1277.6 9.8 reshape.179
  1295.2 12.6 fusion.82
  1307.9 12.4 subtract_bitcast_fusion.1
  1320.3 9.2 copy.38
  1329.4 9.8 reshape.177
  1339.2 46.7 %all-to-all-done.6 = f32[8,1,131072]{2,1,0:T(1,128)} async-done(((f32[8,1,131072]{2,1,0:T(1,128)}), f32[8,1,131072]{2,1,0:T(1,128)}, u32[]{:S(2)}, u32[]{:S(2)}) %all-to-all-start.6) | async-done | bytes 4194336 | tf_op jit(solution)/shard_map/all_to_all | solution.py:146
  1399.0 14.2 reduce.4
  1413.2 8.8 reshape.180
  1422.0 11.5 copy.52
  1441.0 42.1 %all-to-all-done.5 = f32[8,1,131072]{2,1,0:T(1,128)} async-done(((f32[8,1,131072]{2,1,0:T(1,128)}), f32[8,1,131072]{2,1,0:T(1,128)}, u32[]{:S(2)}, u32[]{:S(2)}) %all-to-all-start.5) | async-done | bytes 4194336 | tf_op jit(solution)/shard_map/all_to_all | solution.py:145
  1483.0 13.9 reduce.3
  1496.9 8.8 reshape.178
  1505.7 11.5 copy.53
  1524.9 13.5 fusion.80
  1538.5 21.8 %multiply_add_fusion = (f32[32,64,512]{2,1,0:T(8,128)S(1)}, f32[32,64,512]{2,1,0:T(8,128)}) fusion(f32[32,64,512]{2,1,0:T(8,128)S(1)} %fusion.80, f32[32,64,512]{2,1,0:T(8,128)S(1)} %copy-done.9), kind=kOutput, calls=%fused_computation.110 | convolution fusion | flops 6453460992 | bytes 16777216 | tf_op jit(solution)/shard_map/zxk,ky->zxy/dot_general | solution.py:65
  1591.5 16.5 fusion.39
  1630.7 10.6 fusion.28
  1664.3 11.6 fusion.226
  1675.9 46.5 %psum.7 = f32[]{:T(128)} all-reduce(f32[]{:T(128)} %get-tuple-element.15), channel_id=1, replica_groups=mesh['thick'=4,'wide'=8] {'thick','wide'}, use_global_device_ids=true, to_apply=%region_1.2 | all-reduce | flops 1 | bytes 8 | tf_op jit(solution)/shard_map/psum | solution.py:171
  (133 shorter events, 227.6 us)
Async XLA Ops:
  0.6 4.9 copy-start.4
  3.5 2.0 copy-start.5
  70.0 622.5 %all-to-all-start = ((f32[8,1,262144]{2,1,0:T(1,128)}), f32[8,1,262144]{2,1,0:T(1,128)}, u32[]{:S(2)}, u32[]{:S(2)}) async-start(f32[8,1,262144]{2,1,0:T(1,128)} %reshape.171), calls=%async_computation | async-start | bytes 16777216 | tf_op jit(solution)/shard_map/all_to_all | solution.py:117
  174.5 85.9 %copy-start.11 = (f32[2,32,64,1,64]{4,3,2,1,0:T(1,128)S(1)}, f32[2,32,64,1,64]{4,3,2,1,0:T(1,128)}, u32[]{:S(2)}) copy-start(f32[2,32,64,1,64]{4,3,2,1,0:T(1,128)} %get-tuple-element.8) | copy-start | bytes 3145732
  174.5 85.9 %collective-permute-start = (f32[2,32,64,64]{3,2,1,0:T(8,128)}, f32[2,32,64,64]{3,2,1,0:T(8,128)S(1)}, u32[]{:S(2)}, u32[]{:S(2)}) collective-permute-start(f32[2,32,64,64]{3,2,1,0:T(8,128)} %bitcast.237), channel_id=1, source_target_pairs={{0,1},{1,2},{2,3},{3,4},{4,5},{5,6},{6,7},{7,0},{8,9},{9,10},{10,1... | collective-permute-start | bytes 3145736 | tf_op jit(solution)/shard_map/ppermute | solution.py:34
  176.1 127.3 %collective-permute-start.1 = (f32[2,32,64,64]{3,2,1,0:T(8,128)}, f32[2,32,64,64]{3,2,1,0:T(8,128)S(1)}, u32[]{:S(2)}, u32[]{:S(2)}) collective-permute-start(f32[2,32,64,64]{3,2,1,0:T(8,128)} %bitcast.236), channel_id=1, source_target_pairs={{0,2},{1,3},{2,4},{3,5},{4,6},{5,7},{6,0},{7,1},{8,10},{9,11},{10,... | collective-permute-start | bytes 3145736 | tf_op jit(solution)/shard_map/ppermute | solution.py:34
  177.5 349.6 %collective-permute-start.2 = (f32[2,32,64,64]{3,2,1,0:T(8,128)}, f32[2,32,64,64]{3,2,1,0:T(8,128)S(1)}, u32[]{:S(2)}, u32[]{:S(2)}) collective-permute-start(f32[2,32,64,64]{3,2,1,0:T(8,128)} %bitcast.235), channel_id=1, source_target_pairs={{0,3},{1,4},{2,5},{3,6},{4,7},{5,0},{6,1},{7,2},{8,11},{9,12},{10,... | collective-permute-start | bytes 3145736 | tf_op jit(solution)/shard_map/ppermute | solution.py:34
  178.5 393.6 %collective-permute-start.3 = (f32[2,32,64,64]{3,2,1,0:T(8,128)}, f32[2,32,64,64]{3,2,1,0:T(8,128)S(1)}, u32[]{:S(2)}, u32[]{:S(2)}) collective-permute-start(f32[2,32,64,64]{3,2,1,0:T(8,128)} %bitcast.234), channel_id=1, source_target_pairs={{0,4},{1,5},{2,6},{3,7},{4,0},{5,1},{6,2},{7,3},{8,12},{9,13},{10,... | collective-permute-start | bytes 3145736 | tf_op jit(solution)/shard_map/ppermute | solution.py:34
  181.3 435.6 %collective-permute-start.4 = (f32[2,32,64,64]{3,2,1,0:T(8,128)}, f32[2,32,64,64]{3,2,1,0:T(8,128)S(1)}, u32[]{:S(2)}, u32[]{:S(2)}) collective-permute-start(f32[2,32,64,64]{3,2,1,0:T(8,128)} %bitcast.233), channel_id=1, source_target_pairs={{0,5},{1,6},{2,7},{3,0},{4,1},{5,2},{6,3},{7,4},{8,13},{9,14},{10,... | collective-permute-start | bytes 3145736 | tf_op jit(solution)/shard_map/ppermute | solution.py:34
  182.8 120.6 %copy-start.10 = (f32[2,32,64,1,64]{4,3,2,1,0:T(1,128)S(1)}, f32[2,32,64,1,64]{4,3,2,1,0:T(1,128)}, u32[]{:S(2)}) copy-start(f32[2,32,64,1,64]{4,3,2,1,0:T(1,128)} %get-tuple-element.7) | copy-start | bytes 3145732
  260.4 358.1 %collective-permute-start.5 = (f32[2,32,64,64]{3,2,1,0:T(8,128)S(1)}, f32[2,32,64,64]{3,2,1,0:T(8,128)S(1)}, u32[]{:S(2)}, u32[]{:S(2)}) collective-permute-start(f32[2,32,64,64]{3,2,1,0:T(8,128)S(1)} %bitcast.232), channel_id=1, source_target_pairs={{0,6},{1,7},{2,0},{3,1},{4,2},{5,3},{6,4},{7,5},{8,14},{9,15},{10,... | collective-permute-start | bytes 3145736 | tf_op jit(solution)/shard_map/ppermute | solution.py:34
  303.4 316.5 %collective-permute-start.6 = (f32[2,32,64,64]{3,2,1,0:T(8,128)S(1)}, f32[2,32,64,64]{3,2,1,0:T(8,128)S(1)}, u32[]{:S(2)}, u32[]{:S(2)}) collective-permute-start(f32[2,32,64,64]{3,2,1,0:T(8,128)S(1)} %bitcast.231), channel_id=1, source_target_pairs={{0,7},{1,0},{2,1},{3,2},{4,3},{5,4},{6,5},{7,6},{8,15},{9,8},{10,9... | collective-permute-start | bytes 3145736 | tf_op jit(solution)/shard_map/ppermute | solution.py:34
  825.5 97.7 %all-to-all-start.2 = ((f32[4,1,524288]{2,1,0:T(1,128)}), f32[4,1,524288]{2,1,0:T(1,128)}, u32[]{:S(2)}, u32[]{:S(2)}) async-start(f32[4,1,524288]{2,1,0:T(1,128)} %reshape.175), calls=%async_computation.2 | async-start | bytes 16777216 | tf_op jit(solution)/shard_map/all_to_all | solution.py:126
  923.1 99.0 %all-to-all-start.1 = ((f32[4,1,524288]{2,1,0:T(1,128)}), f32[4,1,524288]{2,1,0:T(1,128)}, u32[]{:S(2)}, u32[]{:S(2)}) async-start(f32[4,1,524288]{2,1,0:T(1,128)} %reshape.173), calls=%async_computation.1 | async-start | bytes 16777216 | tf_op jit(solution)/shard_map/all_to_all | solution.py:125
  1083.2 11.3 copy-start
  1083.2 23.6 %slice-start = ((s8[8388608]{0:T(1024)(128)(4,1)}), s8[4194304]{0:T(1024)(128)(4,1)S(1)}, s32[]{:S(2)}) async-start(s8[8388608]{0:T(1024)(128)(4,1)} %bitcast.205), calls=%async_computation.7 | async-start | bytes 8388608
  1094.5 12.3 slice-start.1
  1106.8 10.4 copy-start.6
  1117.2 5.8 copy-start.7
  1133.9 53.1 %all-to-all-start.4 = ((f32[64,128,128]{2,0,1:T(8,128)}), f32[64,128,128]{2,0,1:T(8,128)}, u32[]{:S(2)}, u32[]{:S(2)}) async-start(f32[64,128,128]{2,0,1:T(8,128)} %copy.36), calls=%async_computation.4 | async-start | bytes 8388608 | tf_op jit(solution)/shard_map/all_to_all | solution.py:140
  1187.0 53.3 %all-to-all-start.3 = ((f32[64,128,128]{2,0,1:T(8,128)}), f32[64,128,128]{2,0,1:T(8,128)}, u32[]{:S(2)}, u32[]{:S(2)}) async-start(f32[64,128,128]{2,0,1:T(8,128)} %copy.34), calls=%async_computation.3 | async-start | bytes 8388608 | tf_op jit(solution)/shard_map/all_to_all | solution.py:139
  1287.4 98.5 %all-to-all-start.6 = ((f32[8,1,131072]{2,1,0:T(1,128)}), f32[8,1,131072]{2,1,0:T(1,128)}, u32[]{:S(2)}, u32[]{:S(2)}) async-start(f32[8,1,131072]{2,1,0:T(1,128)} %reshape.179), calls=%async_computation.6 | async-start | bytes 8388608 | tf_op jit(solution)/shard_map/all_to_all | solution.py:146
  1295.2 12.7 copy-start.1
  1385.9 97.1 %all-to-all-start.5 = ((f32[8,1,131072]{2,1,0:T(1,128)}), f32[8,1,131072]{2,1,0:T(1,128)}, u32[]{:S(2)}, u32[]{:S(2)}) async-start(f32[8,1,131072]{2,1,0:T(1,128)} %reshape.177), calls=%async_computation.5 | async-start | bytes 8388608 | tf_op jit(solution)/shard_map/all_to_all | solution.py:145
  1393.9 4.4 collective-permute-start.7
  1394.0 168.8 %collective-permute-start.8 = (f32[1,64,512]{2,1,0:T(8,128)S(1)}, f32[1,64,512]{2,1,0:T(8,128)S(1)}, u32[]{:S(2)}, u32[]{:S(2)}) collective-permute-start(f32[1,64,512]{2,1,0:T(8,128)S(1)} %get-tuple-element.49), channel_id=1, source_target_pairs={{8,0},{16,8},{24,16},{0,24},{9,1},{17,9},{25,17},{1,25},{10,2},{18... | collective-permute-start | bytes 393224 | tf_op jit(solution)/shard_map/ppermute | solution.py:47
  1524.9 13.5 copy-start.9
  1524.9 37.1 %slice-start.2 = ((s8[4456448]{0:T(1024)(128)(4,1)}), s8[4194304]{0:T(1024)(128)(4,1)S(1)}, s32[]{:S(2)}) async-start(s8[4456448]{0:T(1024)(128)(4,1)} %bitcast.229), calls=%async_computation.9 | async-start | bytes 8388608
  1538.4 23.6 %slice-start.3 = ((s8[4456448]{0:T(1024)(128)(4,1)}), s8[262144]{0:T(1024)(128)(4,1)S(1)}, s32[]{:S(2)}) async-start(s8[4456448]{0:T(1024)(128)(4,1)} %bitcast.229), calls=%async_computation.10 | async-start | bytes 524288
  1538.5 23.6 %copy-start.8 = (f32[32,64,512]{2,1,0:T(8,128)S(1)}, f32[32,64,512]{2,1,0:T(8,128)}, u32[]{:S(2)}) copy-start(f32[32,64,512]{2,1,0:T(8,128)} %param.3) | copy-start | bytes 12582916
  1560.3 4.4 collective-permute-start.11
  1560.3 4.7 collective-permute-start.12
  1565.2 6.2 collective-permute-start.13
  1565.9 6.5 collective-permute-start.14
  1568.9 5.1 collective-permute-start.10
  1570.9 6.0 collective-permute-start.9
  1608.0 13.5 copy-start.2
  1609.1 4.4 collective-permute-start.15
  1609.2 4.5 collective-permute-start.16
  1615.0 5.9 collective-permute-start.17
  1615.1 6.4 collective-permute-start.18
  1641.3 4.4 collective-permute-start.19
  1641.5 4.7 collective-permute-start.20
  1646.3 5.9 collective-permute-start.21
  1646.9 6.5 collective-permute-start.22
  1662.1 2.2 copy-start.3
